TPU v7x, 32 devices: a whole 2x2x4 slice. The times are simulated.
32 devices in a mesh: gx: 4 (over y, core), gy: 8 (over z, x).
Axes of the slice: x: 2, y: 2, z: 4, core: 2. Of those that a mesh axis runs over, the one named last changes fastest.
Arguments:
- perm: float32 [40, 80, 640], P('gx', 'gy'), may hold values from 0.05 to 5
- storage: float32 [40, 80, 640], P('gx', 'gy'), may hold values from 0.2 to 2
- source: float32 [40, 80, 640], P('gx', 'gy'), may hold values from -40 to 40
- weight: float32 [40, 80, 640], P('gx', 'gy'), may hold values from 0.5 to 1.5
- block_map: int32 [40, 80, 640], P('gx', 'gy'), may hold values from 0 to 63, as said below
- coarse_matrix: float32 [27, 4, 8, 64], P(None, 'gx', 'gy'), may hold values from -200 to 2000, as said below
Outputs:
- pressure: float32 [40, 80, 640], P('gx', 'gy')
- final_residual: float32 [40, 80, 640], P('gx', 'gy')
Inputs may be any that keep to these rules, and one draw needn't show every extreme that they name: `block_map`: each cell's number l names a coarse block of its own device's brick of 10 x 10 x 640 cells, naming the l-th block of 10 cells along z inside the brick: the block that contains the cell, or, for a cell on the first layer of a block along a dimension that is not the brick's face, possibly the previous block along that dimension. `coarse_matrix`: for every block, entry 13 is positive and larger than the sum of the magnitudes of the other 26 entries; the other entries are zero or negative, zero where the offset leaves the block grid, and entry o at a block equals entry 26 - o at the block shifted by offset o.
All inputs are finite; a program needn't handle non-finite values.
Results may differ from a plain program's by a relative error of at most 0.0003.
Values sent between devices are 32-bit elements; how exact they have to be, the bound alone decides.
A program may use at most 64 MiB of HBM per device.

v0:
```python
import jax
import jax.numpy as jnp
from jax import lax
from jax.sharding import PartitionSpec as P

ITERS = 6


OMEGA = 0.8


def padded_2(shard, sides, width):
    for axis, dim in sides:
        count, length = (lax.axis_size(axis), shard.shape[dim])
        up = [(i, (i + 1) % count) for i in range(count - 1)]
        down = [(j, i) for i, j in up]
        last = lax.slice_in_dim(shard, length - width, length, axis=dim)
        initial = lax.slice_in_dim(shard, 0, width, axis=dim)
        before = lax.ppermute(last, axis, up)
        after = lax.ppermute(initial, axis, down)
        shard = jnp.concatenate([before, shard, after], axis=dim)
    return shard


def harmonic(cell_perm, other_perm):
    total = cell_perm + other_perm
    return 2.0 * cell_perm * other_perm / jnp.where(total > 0.0, total, 1.0)


def face_terms(padded):
    center = padded[1:-1, 1:-1, 1:-1]
    return (
        harmonic(center, padded[2:, 1:-1, 1:-1]),
        harmonic(center, padded[:-2, 1:-1, 1:-1]),
        harmonic(center, padded[1:-1, 2:, 1:-1]),
        harmonic(center, padded[1:-1, :-2, 1:-1]),
        harmonic(center, padded[1:-1, 1:-1, 2:]),
        harmonic(center, padded[1:-1, 1:-1, :-2]),
    )


def diagonal_of(face_list, storage):
    return storage + (
        face_list[0] + face_list[1] + face_list[2] + face_list[3] + face_list[4] + face_list[5]
    )


def neighbour_flux(face_list, padded):
    summed = face_list[0] * padded[2:, 1:-1, 1:-1] + face_list[1] * padded[:-2, 1:-1, 1:-1]
    summed = summed + face_list[2] * padded[1:-1, 2:, 1:-1] + face_list[3] * padded[1:-1, :-2, 1:-1]
    summed = summed + face_list[4] * padded[1:-1, 1:-1, 2:] + face_list[5] * padded[1:-1, 1:-1, :-2]
    return summed


def coarse_apply(matrix, padded):
    extent = matrix.shape[1:]
    summed = jnp.zeros(extent, jnp.float32)
    for offset in range(27):
        shift_x = offset // 9
        shift_y = offset // 3 % 3
        shift_z = offset % 3
        summed = (
            summed
            + matrix[offset]
            * padded[
                shift_x : shift_x + extent[0],
                shift_y : shift_y + extent[1],
                shift_z : shift_z + extent[2],
            ]
        )
    return summed


def conjugate(matrix, coarse_rhs, pad_field, norm_sum, curve_sum):
    solution = jnp.zeros_like(coarse_rhs)
    residual = coarse_rhs
    direction = coarse_rhs
    norm_now = norm_sum(jnp.sum(residual * residual))
    for iteration in range(ITERS):
        applied = coarse_apply(matrix, pad_field(direction))
        step_size = norm_now / curve_sum(jnp.sum(direction * applied))
        solution = solution + step_size * direction
        residual = residual - step_size * applied
        if iteration + 1 < ITERS:
            norm_next = norm_sum(jnp.sum(residual * residual))
            direction = residual + norm_next / norm_now * direction
            norm_now = norm_next
    return solution


def squares(values):
    return lax.psum(values, ("gx", "gy"))


def curving(values):
    return lax.psum(values, ("gx", "gy"))


def block_sums(values, block_map, blocks):
    labels = jnp.arange(blocks, dtype=jnp.int32)
    slab_values = values.reshape(values.shape[0], -1)
    slab_maps = block_map.reshape(block_map.shape[0], -1)

    def accumulate(total, pair):
        indicator = (pair[1][:, None] == labels[None, :]).astype(jnp.float32)
        return (total + jnp.dot(pair[0], indicator, precision=lax.Precision.HIGHEST), None)

    total, unused = lax.scan(
        accumulate, jnp.zeros((blocks,), jnp.float32), (slab_values, slab_maps)
    )
    return total


def block_spread(correction, block_map):
    blocks = correction.shape[0]
    labels = jnp.arange(blocks, dtype=jnp.int32)
    slab_maps = block_map.reshape(block_map.shape[0], -1)

    def expand(carry, slab):
        indicator = (slab[:, None] == labels[None, :]).astype(jnp.float32)
        return (carry, jnp.dot(indicator, correction, precision=lax.Precision.HIGHEST))

    unused, spread = lax.scan(expand, jnp.int32(0), slab_maps)
    return spread.reshape(block_map.shape)


def shards(perm, storage, source, weight, block_map, coarse_matrix):
    z_padding = ((0, 0), (0, 0), (1, 1))
    padded_perm = jnp.pad(padded_2(perm, (("gx", 0), ("gy", 1)), 1), z_padding)
    face_list = face_terms(padded_perm)
    diagonal = diagonal_of(face_list, storage)

    def operate_step(values):
        padded = jnp.pad(padded_2(values, (("gx", 0), ("gy", 1)), 1), z_padding)
        return diagonal * values - neighbour_flux(face_list, padded)

    sweep_one = OMEGA * source / diagonal
    second = sweep_one + OMEGA * (source - operate_step(sweep_one)) / diagonal
    fine_residual = source - operate_step(second)

    def pad_halo(values):
        return jnp.pad(padded_2(values, (("gx", 0), ("gy", 1)), 1), z_padding)

    extent = coarse_matrix.shape[1:]
    blocks = extent[0] * extent[1] * extent[2]
    coarse_rhs = block_sums(weight * fine_residual, block_map, blocks).reshape(extent)
    correction = conjugate(coarse_matrix, coarse_rhs, pad_halo, squares, curving)
    pressure = second + weight * block_spread(correction.reshape(-1), block_map)
    padded_pressure = jnp.pad(padded_2(pressure, (("gx", 0), ("gy", 1)), 1), z_padding)
    final_residual = source - (diagonal * pressure - neighbour_flux(face_list, padded_pressure))
    return (pressure, final_residual)


def solution(mesh):
    placed = (
        P("gx", "gy", None),
        P("gx", "gy", None),
        P("gx", "gy", None),
        P("gx", "gy", None),
        P("gx", "gy", None),
        P(None, "gx", "gy", None),
    )
    return jax.shard_map(
        shards,
        mesh=mesh,
        in_specs=placed,
        out_specs=(P("gx", "gy", None), P("gx", "gy", None)),
        check_vma=False,
    )
```

profile of v0, /device:TPU:0, one launch (start us, length us, event | category | flops | bytes accessed | tf_op | source)
XLA Modules:
  0.0 701.1 jit_solution(7355788932985097275)
XLA Ops:
  10.4 4.5 collective-permute-start.3
  25.4 4.9 collective-permute-start.7
  40.8 5.5 collective-permute-start.11
  50.8 28.6 %while.23 = (s32[]{:T(128)}, f32[64]{0:T(128)S(1)}, f32[10,6400]{1,0:T(8,128)}, s32[10,6400]{1,0:T(8,128)}, s32[]{:T(128)}, /*index=5*/s32[]{:T(128)}) while((s32[]{:T(128)}, f32[64]{0:T(128)S(1)}, f32[10,6400]{1,0:T(8,128)}, s32[10,6400]{1,0:T(8,128)}, s32[]{:T(128)}, /*index=5*/s32[]{:T(128)}) %tuple.72), condition=%wide.region_1.2_spmd.clone, body=%wide.region_0.1_spmd.clone.sunk | while | flops 5324931 | bytes 103507 | solution.py:108
  79.3 5.0 collective-permute-start.12
  89.5 5.1 collective-permute-start.14
  101.1 43.9 %all-reduce.10 = (f32[]{:T(128)}, f32[]{:T(128)}) all-reduce(f32[]{:T(128)} %multiply_reduce_fusion.10, f32[]{:T(128)} %get-tuple-element.119), channel_id=1, replica_groups=mesh['gx'=4,'gy'=8] {'gx','gy'}, use_global_device_ids=true, to_apply=%region_3.4 | all-reduce | flops 2 | bytes 16 | tf_op jit(solution)/shard_map/psum | solution.py:92
  147.0 38.9 %psum.86 = f32[]{:T(128)} all-reduce(f32[]{:T(128)} %get-tuple-element.117), channel_id=1, replica_groups=mesh['gx'=4,'gy'=8] {'gx','gy'}, use_global_device_ids=true, to_apply=%region_7.8 | all-reduce | flops 1 | bytes 8 | tf_op jit(solution)/shard_map/psum | solution.py:92
  189.9 4.4 collective-permute-done.17
  204.1 42.1 %psum.87 = f32[]{:T(128)} all-reduce(f32[]{:T(128)} %get-tuple-element.115), channel_id=1, replica_groups=mesh['gx'=4,'gy'=8] {'gx','gy'}, use_global_device_ids=true, to_apply=%region_9.10 | all-reduce | flops 1 | bytes 8 | tf_op jit(solution)/shard_map/psum | solution.py:96
  248.1 39.2 %psum.88 = f32[]{:T(128)} all-reduce(f32[]{:T(128)} %get-tuple-element.113), channel_id=1, replica_groups=mesh['gx'=4,'gy'=8] {'gx','gy'}, use_global_device_ids=true, to_apply=%region_11.12 | all-reduce | flops 1 | bytes 8 | tf_op jit(solution)/shard_map/psum | solution.py:92
  291.2 4.4 collective-permute-done.21
  305.7 41.5 %psum.89 = f32[]{:T(128)} all-reduce(f32[]{:T(128)} %get-tuple-element.111), channel_id=1, replica_groups=mesh['gx'=4,'gy'=8] {'gx','gy'}, use_global_device_ids=true, to_apply=%region_13.14 | all-reduce | flops 1 | bytes 8 | tf_op jit(solution)/shard_map/psum | solution.py:96
  349.0 39.3 %psum.90 = f32[]{:T(128)} all-reduce(f32[]{:T(128)} %get-tuple-element.109), channel_id=1, replica_groups=mesh['gx'=4,'gy'=8] {'gx','gy'}, use_global_device_ids=true, to_apply=%region_15.16 | all-reduce | flops 1 | bytes 8 | tf_op jit(solution)/shard_map/psum | solution.py:92
  392.1 4.4 collective-permute-done.25
  406.7 40.8 %psum.91 = f32[]{:T(128)} all-reduce(f32[]{:T(128)} %get-tuple-element.107), channel_id=1, replica_groups=mesh['gx'=4,'gy'=8] {'gx','gy'}, use_global_device_ids=true, to_apply=%region_17.18 | all-reduce | flops 1 | bytes 8 | tf_op jit(solution)/shard_map/psum | solution.py:96
  449.4 39.9 %psum.92 = f32[]{:T(128)} all-reduce(f32[]{:T(128)} %get-tuple-element.105), channel_id=1, replica_groups=mesh['gx'=4,'gy'=8] {'gx','gy'}, use_global_device_ids=true, to_apply=%region_19.20 | all-reduce | flops 1 | bytes 8 | tf_op jit(solution)/shard_map/psum | solution.py:92
  493.3 4.5 collective-permute-done.29
  507.8 40.6 %psum.93 = f32[]{:T(128)} all-reduce(f32[]{:T(128)} %get-tuple-element.103), channel_id=1, replica_groups=mesh['gx'=4,'gy'=8] {'gx','gy'}, use_global_device_ids=true, to_apply=%region_21.22 | all-reduce | flops 1 | bytes 8 | tf_op jit(solution)/shard_map/psum | solution.py:96
  550.4 40.1 %psum.94 = f32[]{:T(128)} all-reduce(f32[]{:T(128)} %multiply_reduce_fusion), channel_id=1, replica_groups=mesh['gx'=4,'gy'=8] {'gx','gy'}, use_global_device_ids=true, to_apply=%region_23.24 | all-reduce | flops 1 | bytes 8 | tf_op jit(solution)/shard_map/psum | solution.py:92
  594.4 4.4 collective-permute-done.33
  608.6 40.2 %psum.95 = f32[]{:T(128)} all-reduce(f32[]{:T(128)} %fusion.222), channel_id=1, replica_groups=mesh['gx'=4,'gy'=8] {'gx','gy'}, use_global_device_ids=true, to_apply=%region_25.26 | all-reduce | flops 1 | bytes 8 | tf_op jit(solution)/shard_map/psum | solution.py:96
  650.1 33.2 %while.22 = (s32[]{:T(128)}, f32[10,6400]{1,0:T(8,128)}, s32[10,6400]{1,0:T(8,128)}, f32[64]{0:T(128)S(1)}, s32[]{:T(128)}, /*index=5*/s32[]{:T(128)}) while((s32[]{:T(128)}, f32[10,6400]{1,0:T(8,128)}, s32[10,6400]{1,0:T(8,128)}, f32[64]{0:T(128)S(1)}, s32[]{:T(128)}, /*index=5*/s32[]{:T(128)}) %tuple.70), condition=%wide.region_27.28_spmd.clone, body=%wide.region_26.27_spmd.clone.sunk | while | flops 5324802 | bytes 153933 | solution.py:123
  692.9 4.8 collective-permute-start.39
  (190 shorter events, 186.6 us)
Async XLA Ops:
  3.8 5.2 collective-permute-start
  9.1 5.9 collective-permute-start.2
  10.4 6.1 collective-permute-start.3
  17.8 5.4 collective-permute-start.4
  24.1 6.2 collective-permute-start.6
  25.4 6.5 collective-permute-start.7
  39.5 8.7 %collective-permute-start.10 = (f32[12,1,640]{2,1,0:T(1,128)}, f32[12,1,640]{2,1,0:T(1,128)S(1)}, u32[]{:S(2)}, u32[]{:S(2)}) collective-permute-start(f32[12,1,640]{2,1,0:T(1,128)} %get-tuple-element.129), channel_id=1, source_target_pairs={{1,0},{2,1},{3,2},{4,3},{5,4},{6,5},{7,6},{9,8},{10,9},{11,10},{12... | collective-permute-start | bytes 92168 | tf_op jit(solution)/shard_map/ppermute | solution.py:20
  40.8 7.4 %collective-permute-start.11 = (f32[12,1,640]{2,1,0:T(1,128)S(1)}, f32[12,1,640]{2,1,0:T(1,128)S(1)}, u32[]{:S(2)}, u32[]{:S(2)}) collective-permute-start(f32[12,1,640]{2,1,0:T(1,128)S(1)} %get-tuple-element.128), channel_id=1, source_target_pairs={{0,1},{1,2},{2,3},{3,4},{4,5},{5,6},{6,7},{8,9},{9,10},{10,11},{11... | collective-permute-start | bytes 92168 | tf_op jit(solution)/shard_map/ppermute | solution.py:19
  79.3 6.3 collective-permute-start.12
  84.4 5.1 collective-permute-start.13
  89.5 7.1 %collective-permute-start.14 = (f32[3,1,64]{2,1,0:T(1,128)S(1)}, f32[3,1,64]{2,1,0:T(1,128)S(1)}, u32[]{:S(2)}, u32[]{:S(2)}) collective-permute-start(f32[3,1,64]{2,1,0:T(1,128)S(1)} %pad_maximum_fusion.37), channel_id=1, source_target_pairs={{0,1},{1,2},{2,3},{3,4},{4,5},{5,6},{6,7},{8,9},{9,10},{10,11},{11... | collective-permute-start | bytes 2312 | tf_op jit(solution)/shard_map/ppermute | solution.py:19
  94.6 5.7 collective-permute-start.15
  188.6 5.7 collective-permute-start.17
  197.7 5.5 collective-permute-start.19
  289.9 5.7 collective-permute-start.21
  299.4 5.5 collective-permute-start.23
  390.8 5.7 collective-permute-start.25
  400.4 5.5 collective-permute-start.27
  492.0 5.8 collective-permute-start.29
  501.5 5.5 collective-permute-start.31
  593.1 5.7 collective-permute-start.33
  602.4 5.5 collective-permute-start.35
  691.6 6.1 collective-permute-start.38
  692.9 6.4 collective-permute-start.39
  (23 other events, 161.2 us)
where the time goes:
time: 707 us; the launch traced here: 701 us
  blocking collectives  447 us (63%)
  starting transfers between devices  93.5 us (13%)
  waiting for transfers between devices  60.5 us (9%)
  local copies, waits for them, and re-layouts  44.4 us (6%)
  matrix products  24.2 us (3%)
  other arithmetic  15.8 us (2%)
  between operations  15.7 us (2%)
    psum x6, blocking collectives, squares(): return lax.psum(values, ('gx', 'gy'))  241 us
    psum x5, blocking collectives, curving(): return lax.psum(values, ('gx', 'gy'))  205 us
    ppermute x20, starting transfers between devices, padded_2(): before = lax.ppermute(last, axis, up)  67.7 us
    ppermute x20, waiting for transfers between devices, padded_2(): after = lax.ppermute(initial, axis, down)  53.3 us
    ppermute x20, starting transfers between devices, padded_2(): after = lax.ppermute(initial, axis, down)  25.8 us
    dynamic_slice x20, local copies, waits for them, and re-layouts, block_sums(): lax.scan(accumulate, jnp.zeros((blocks,), jnp.float32), (slab_values, sla...  20.2 us
    dot_general x10, matrix products, accumulate(): jnp.dot(pair[0], indicator, precision=lax.Precision.HIGHEST)  18.2 us
    dynamic_update_slice x10, local copies, waits for them, and re-layouts, block_spread(): unused, spread = lax.scan(expand, jnp.int32(0), slab_maps)  17.1 us
  transfers between devices with their start and end apart: 40, of which 19 were waited for; matrix products, arithmetic and copies ran while one was open for 1% of the time, Pallas kernels for 0%

commit v1 on v0

v1 whole, which is shorter than its diff:
```python
import functools

import jax
import jax.numpy as jnp
from jax import lax
from jax.experimental import pallas as pl
from jax.experimental.pallas import tpu as pltpu
from jax.sharding import PartitionSpec as P

ITERS = 6
OMEGA = 0.8
MESH = pl.DeviceIdType.MESH
F32 = jnp.float32


def harmonic(a, b):
    return 2.0 * a * b / (a + b)


def pieces(value):
    high = value.astype(jnp.bfloat16).astype(F32)
    rest = value - high
    middle = rest.astype(jnp.bfloat16).astype(F32)
    return high, middle, rest - middle


def kernel(
    ngx, ngy, block,
    perm_h, storage_h, source_h, weight_h, map_h, matrix_h,
    pressure_h, final_h,
    perm_v, storage_v, source_v, weight_v, map_v, matrix_v,
    pad_p, v1, v2, tx, typ, tym, tzp, tzm, diag, inv,
    sy, ry, sx, sym, rym, px, wx, mx,
    tile, gm, coef, row, gr, field, spread, ind, indt,
    pressure_v, final_v,
    local_sem, send_sem, recv_sem, gsend_sem, grecv_sem,
):
    n = ngx * ngy
    cx, cy, nz = perm_v.shape
    blocks = matrix_v.shape[-1]
    gx, gy = lax.axis_index("gx"), lax.axis_index("gy")
    me = gx * ngy + gy
    has = (gy > 0, gy < ngy - 1, gx > 0, gx < ngx - 1)
    near = ((gx, gy - 1), (gx, gy + 1), (gx - 1, gy), (gx + 1, gy))

    loads = [
        pltpu.make_async_copy(src, dst, local_sem.at[i])
        for i, (src, dst) in enumerate((
            (perm_h, perm_v), (matrix_h, matrix_v), (source_h, source_v),
            (storage_h, storage_v), (weight_h, weight_v), (map_h, map_v),
        ))
    ]
    for load in loads:
        load.start()

    def other(k):
        t = lax.rem(me + k, n)
        return (t // ngy, lax.rem(t, ngy))

    barrier = pltpu.get_barrier_semaphore()

    @pl.loop(1, n)
    def _(k):
        pl.semaphore_signal(barrier, inc=1, device_id=other(k), device_id_type=MESH)

    for d in range(2):
        @pl.when(jnp.logical_not(has[d]))
        def _():
            for s in range(4):
                ry[s, d] = jnp.zeros(ry.shape[2:], F32)
            rym[d] = jnp.zeros(rym.shape[1:], jnp.int32)

        @pl.when(jnp.logical_not(has[2 + d]))
        def _():
            px[d] = jnp.zeros(px.shape[1:], F32)
            wx[d] = jnp.zeros(wx.shape[1:], F32)
            mx[d] = jnp.zeros(mx.shape[1:], jnp.int32)
            for v in (v1, v2):
                v[d * (cx + 1)] = jnp.zeros(v.shape[1:], F32)

    zid = lax.broadcasted_iota(jnp.int32, (nz, 128), 0) // block
    ind[...] = (zid == lax.broadcasted_iota(jnp.int32, (nz, 128), 1)).astype(F32).astype(jnp.bfloat16)
    zidt = lax.broadcasted_iota(jnp.int32, (128, nz), 1) // block
    indt[...] = (zidt == lax.broadcasted_iota(jnp.int32, (128, nz), 0)).astype(F32).astype(jnp.bfloat16)
    pad_p[...] = jnp.ones(pad_p.shape, F32)
    tile[...] = jnp.zeros(tile.shape, F32)
    sx[...] = jnp.zeros(sx.shape, F32)

    pl.semaphore_wait(barrier, n - 1)

    def halo(stage, d, src, dst):
        return pltpu.make_async_remote_copy(
            src_ref=src, dst_ref=dst,
            send_sem=send_sem.at[stage * 4 + d],
            recv_sem=recv_sem.at[stage * 4 + (d ^ 1)],
            device_id=near[d], device_id_type=MESH,
        )

    def send(stage, d, src, dst):
        @pl.when(has[d])
        def _():
            halo(stage, d, src, dst).start()

    def wait_sent(stage, d, src, dst):
        @pl.when(has[d])
        def _():
            halo(stage, d, src, dst).wait_send()

    def wait_halo(stage, d, dst):
        @pl.when(has[d])
        def _():
            pltpu.make_async_remote_copy(
                src_ref=dst, dst_ref=dst,
                send_sem=send_sem.at[stage * 4 + d],
                recv_sem=recv_sem.at[stage * 4 + d],
                device_id=near[d], device_id_type=MESH,
            ).wait_recv()

    sent = []

    def go(stage, d, src, dst):
        send(stage, d, src, dst)
        sent.append((stage, d, src, dst))

    for d in range(2):
        go(0, 2 + d, perm_h.at[(cx - 1) * d], px.at[d ^ 1])
    loads[0].wait()

    @pl.loop(0, cx)
    def _(x):
        p = perm_v[x]
        pad_p[x + 1, 0:cy] = p
        sy[0, 0, pl.ds(x, 1)] = p[0:1]
        sy[0, 1, pl.ds(x, 1)] = p[cy - 1 : cy]

    for d in range(2):
        go(0, d, sy.at[0, d], ry.at[0, d ^ 1])

    loads[1].wait()
    for p in range(7):
        tile[p : p + 1, 0:blocks] = matrix_v[p, 0]
        tile[p : p + 1, 64 : 64 + blocks] = matrix_v[p + 7, 0]

    def matrix_copy(k):
        return pltpu.make_async_remote_copy(
            src_ref=tile, dst_ref=gm.at[pl.ds(pl.multiple_of(me * 8, 8), 8)],
            send_sem=gsend_sem.at[0], recv_sem=grecv_sem.at[0],
            device_id=other(k), device_id_type=MESH,
        )

    loads[4].wait()
    loads[5].wait()

    @pl.loop(0, cx)
    def _(x):
        w = weight_v[x]
        sy[3, 0, pl.ds(x, 1)] = w[0:1]
        sy[3, 1, pl.ds(x, 1)] = w[cy - 1 : cy]
        m = map_v[x]
        sym[0, pl.ds(x, 1)] = m[0:1]
        sym[1, pl.ds(x, 1)] = m[cy - 1 : cy]

    loads[2].wait()
    loads[3].wait()

    for d in range(4):
        wait_halo(0, d, ry.at[0, d] if d < 2 else px.at[d - 2])

    def to_rows(buffer, stage):
        @pl.loop(0, cx)
        def _(x):
            buffer[x + 1, 15:16] = ry[stage, 0, pl.ds(x, 1)]
            buffer[x + 1, cy : cy + 1] = ry[stage, 1, pl.ds(x, 1)]

    pad_p[0, 0:cy] = px[0]
    pad_p[cx + 1, 0:cy] = px[1]
    to_rows(pad_p, 0)

    tx[0] = harmonic(pad_p[0], pad_p[1])
    lane = lax.broadcasted_iota(jnp.int32, (16, nz), 1)

    @pl.loop(0, cx)
    def _(x):
        p = pad_p[x + 1]
        up = harmonic(p, pad_p[x + 2])
        tx[x + 1] = up
        yp = harmonic(p, pltpu.roll(p, 15, 0))
        ym = pltpu.roll(yp, 1, 0)
        zp = jnp.where(lane == nz - 1, 0.0, harmonic(p, pltpu.roll(p, nz - 1, 1)))
        zm = pltpu.roll(zp, 1, 1)
        typ[x] = yp[0:cy]
        tym[x] = ym[0:cy]
        tzp[x] = zp[0:cy]
        tzm[x] = zm[0:cy]
        total = storage_v[x] + (up + tx[x] + yp + ym + zp + zm)[0:cy]
        inverse = 1.0 / total
        diag[x] = total
        inv[x] = inverse
        first = OMEGA * source_v[x] * inverse
        v1[x + 1, 0:cy] = first
        sy[1, 0, pl.ds(x, 1)] = first[0:1]
        sy[1, 1, pl.ds(x, 1)] = first[cy - 1 : cy]

    def field_halo(stage, v):
        for d in range(2):
            go(stage, d, sy.at[stage, d], ry.at[stage, d ^ 1])
        for d in range(2):
            sx[stage - 1, d, 0:cy] = v[1 + (cx - 1) * d, 0:cy]
            go(stage, 2 + d, sx.at[stage - 1, d], v.at[(cx + 1) * (1 - d)])

    def field_wait(stage, v):
        for d in range(4):
            wait_halo(stage, d, ry.at[stage, d] if d < 2 else v.at[(cx + 1) * (d - 2)])

    def operate(v, x):
        c = v[x + 1]
        total = tx[x + 1, 0:cy] * v[x + 2, 0:cy] + tx[x, 0:cy] * v[x, 0:cy]
        total += typ[x] * pltpu.roll(c, 15, 0)[0:cy] + tym[x] * pltpu.roll(c, 1, 0)[0:cy]
        total += tzp[x] * pltpu.roll(c, nz - 1, 1)[0:cy] + tzm[x] * pltpu.roll(c, 1, 1)[0:cy]
        return c[0:cy], diag[x] * c[0:cy] - total

    field_halo(1, v1)

    @pl.loop(1, n)
    def _(k):
        matrix_copy(k).start()

    gm[pl.ds(pl.multiple_of(me * 8, 8), 8)] = tile[...]

    field_wait(1, v1)
    to_rows(v1, 1)

    @pl.loop(0, cx)
    def _(x):
        c, image = operate(v1, x)
        second = c + OMEGA * (source_v[x] - image) * inv[x]
        v2[x + 1, 0:cy] = second
        sy[2, 0, pl.ds(x, 1)] = second[0:1]
        sy[2, 1, pl.ds(x, 1)] = second[cy - 1 : cy]

    field_halo(2, v2)

    for d in range(2):
        go(3, d, sy.at[3, d], ry.at[3, d ^ 1])
        go(4, d, sym.at[d], rym.at[d ^ 1])
        go(3, 2 + d, weight_h.at[(cx - 1) * d], wx.at[d ^ 1])
        go(4, 2 + d, map_h.at[(cx - 1) * d], mx.at[d ^ 1])

    field_wait(2, v2)
    to_rows(v2, 2)

    zblock = lax.broadcasted_iota(jnp.int32, (cy, nz), 1) // block

    def gather(x, carry):
        same, before = carry
        c, image = operate(v2, x)
        value = weight_v[x] * (source_v[x] - image)
        here = map_v[x] == zblock
        return same + jnp.where(here, value, 0.0), before + jnp.where(here, 0.0, value)

    zero = jnp.zeros((cy, nz), F32)
    same, before = lax.fori_loop(0, cx, gather, (zero, zero))
    same = jnp.broadcast_to(jnp.sum(same, axis=0, keepdims=True), (16, nz))
    before = jnp.broadcast_to(jnp.sum(before, axis=0, keepdims=True), (16, nz))
    high, middle, low = pieces(same + pltpu.roll(before, nz - 1, 1))
    rows = lax.broadcasted_iota(jnp.int32, (16, nz), 0)
    stacked = jnp.where(rows == 0, high, jnp.where(rows == 1, middle, jnp.where(rows == 2, low, 0.0)))
    sums = jnp.dot(stacked.astype(jnp.bfloat16), ind[...], preferred_element_type=F32)
    mine = jnp.sum(sums, axis=0, keepdims=True)
    row[...] = mine

    def row_copy(k):
        return pltpu.make_async_remote_copy(
            src_ref=row, dst_ref=gr.at[me],
            send_sem=gsend_sem.at[1], recv_sem=grecv_sem.at[1],
            device_id=other(k), device_id_type=MESH,
        )

    @pl.loop(1, n)
    def _(k):
        row_copy(k).start()

    gr[me] = mine

    def all_of(buffer, size, which):
        part = buffer.at[pl.ds(0, size)]
        return pltpu.make_async_remote_copy(
            src_ref=part, dst_ref=part,
            send_sem=gsend_sem.at[which], recv_sem=grecv_sem.at[which],
            device_id=other(1), device_id_type=MESH,
        )

    all_of(gm, (n - 1) * 8, 0).wait_recv()
    lower = lax.broadcasted_iota(jnp.int32, (ngy, 128), 1) < 64
    for p in range(7):
        for g in range(ngx):
            both = gm[pl.ds(g * ngy * 8 + p, ngy, stride=8), :]
            coef[p, g] = jnp.where(lower, both, 0.0)
            coef[p + 7, g] = jnp.where(lower, pltpu.roll(both, 64, 1), 0.0)

    def moved(plane, dy, dz):
        if dz:
            plane = pltpu.roll(plane, dz % 128, 1)
        if dy:
            plane = pltpu.roll(plane, dy % ngy, 0)
        return plane

    for o in range(13):
        dx, dy, dz = o // 9 - 1, o // 3 % 3 - 1, o % 3 - 1
        for g in range(ngx):
            coef[26 - o, g] = moved(coef[o, (g - dx) % ngx], dy, dz)

    all_of(gr, n - 1, 1).wait_recv()
    for g in range(ngx):
        for h in range(ngy):
            field[g, h : h + 1] = gr[g * ngy + h]

    def apply(u):
        result = [None] * ngx
        for dy in (-1, 0, 1):
            for dz in (-1, 0, 1):
                shifted = [moved(plane, -dy, -dz) for plane in u]
                for dx in (-1, 0, 1):
                    o = 9 * (dx + 1) + 3 * (dy + 1) + dz + 1
                    for g in range(ngx):
                        if 0 <= g + dx < ngx:
                            term = coef[o, g] * shifted[g + dx]
                            result[g] = term if result[g] is None else result[g] + term
        return result

    def inner(a, b):
        total = a[0] * b[0]
        for g in range(1, ngx):
            total = total + a[g] * b[g]
        return jnp.sum(jnp.sum(total, axis=0, keepdims=True), axis=1, keepdims=True)

    residual = [field[g] for g in range(ngx)]
    direction = residual
    answer = [jnp.zeros((ngy, 128), F32)] * ngx
    norm = inner(residual, residual)
    for iteration in range(ITERS):
        applied = apply(direction)
        step = norm / inner(direction, applied)
        answer = [a + step * b for a, b in zip(answer, direction)]
        if iteration + 1 < ITERS:
            residual = [a - step * b for a, b in zip(residual, applied)]
            following = inner(residual, residual)
            ratio = following / norm
            direction = [a + ratio * b for a, b in zip(residual, direction)]
            norm = following
    for g in range(ngx):
        field[g] = answer[g]

    west, east = jnp.maximum(gx - 1, 0), jnp.minimum(gx + 1, ngx - 1)
    south, north = jnp.maximum(gy - 1, 0), jnp.minimum(gy + 1, ngy - 1)
    picks = ((gx, gy), (gx, south), (gx, north), (west, gy), (east, gy))
    rows = lax.broadcasted_iota(jnp.int32, (16, 128), 0)
    stacked = jnp.zeros((16, 128), F32)
    for i, (a, b) in enumerate(picks):
        value = jnp.broadcast_to(field[a, pl.ds(b, 1)], (16, 128))
        for j, piece in enumerate(pieces(value)):
            stacked = jnp.where(rows == 3 * i + j, piece, stacked)
    spread[...] = jnp.dot(stacked.astype(jnp.bfloat16), indt[...], preferred_element_type=F32)

    def by_block(i):
        value = spread[3 * i : 3 * i + 1] + spread[3 * i + 1 : 3 * i + 2] + spread[3 * i + 2 : 3 * i + 3]
        value = jnp.broadcast_to(value, (16, nz))
        return value[0:cy], pltpu.roll(value, 1, 1)[0:cy]

    for d in range(4):
        wait_halo(3, d, ry.at[3, d] if d < 2 else wx.at[d - 2])
        wait_halo(4, d, rym.at[d] if d < 2 else mx.at[d - 2])

    for d in range(2):
        now, prior = by_block(1 + d)
        ry[2, d] = ry[2, d] + ry[3, d] * jnp.where(rym[d] == zblock, now, prior)
        now, prior = by_block(3 + d)
        at = d * (cx + 1)
        v1[at, 0:cy] = v2[at, 0:cy] + wx[d] * jnp.where(mx[d] == zblock, now, prior)

    now, prior = by_block(0)

    @pl.loop(0, cx)
    def _(x):
        value = v2[x + 1, 0:cy] + weight_v[x] * jnp.where(map_v[x] == zblock, now, prior)
        pressure_v[x] = value

    out = pltpu.make_async_copy(pressure_v, pressure_h, local_sem.at[6])
    out.start()
    for item in sent:
        wait_sent(*item)

    @pl.loop(0, cx)
    def _(x):
        v1[x + 1, 0:cy] = pressure_v[x]

    to_rows(v1, 2)

    @pl.loop(0, cx)
    def _(x):
        c, image = operate(v1, x)
        final_v[x] = source_v[x] - image

    out2 = pltpu.make_async_copy(final_v, final_h, local_sem.at[7])
    out2.start()
    all_of(gm, (n - 1) * 8, 0).wait_send()
    all_of(gr, n - 1, 1).wait_send()
    out.wait()
    out2.wait()


def solution(mesh):
    ngx, ngy = mesh.shape["gx"], mesh.shape["gy"]

    def shards(perm, storage, source, weight, block_map, matrix):
        cx, cy, nz = perm.shape
        block = nz // matrix.shape[-1]
        n = ngx * ngy
        brick = pltpu.VMEM((cx, cy, nz), F32)
        padded = pltpu.VMEM((cx + 2, 16, nz), F32)
        face = pltpu.VMEM((2, cy, nz), F32)
        shape = jax.ShapeDtypeStruct(perm.shape, F32)
        return pl.pallas_call(
            functools.partial(kernel, ngx, ngy, block),
            out_shape=(shape, shape),
            in_specs=[pl.BlockSpec(memory_space=pltpu.HBM)] * 6,
            out_specs=[pl.BlockSpec(memory_space=pltpu.HBM)] * 2,
            scratch_shapes=[
                brick, brick, brick, brick, pltpu.VMEM((cx, cy, nz), jnp.int32),
                pltpu.VMEM(matrix.shape, F32),
                padded, padded, padded, pltpu.VMEM((cx + 1, 16, nz), F32),
                brick, brick, brick, brick, brick, brick,
                pltpu.VMEM((4, 2, cx, nz), F32), pltpu.VMEM((4, 2, cx, nz), F32),
                pltpu.VMEM((2, 2, 16, nz), F32),
                pltpu.VMEM((2, cx, nz), jnp.int32), pltpu.VMEM((2, cx, nz), jnp.int32),
                face, face, pltpu.VMEM((2, cy, nz), jnp.int32),
                pltpu.VMEM((8, 128), F32), pltpu.VMEM((n * 8, 128), F32),
                pltpu.VMEM((27, ngx, ngy, 128), F32),
                pltpu.VMEM((1, 128), F32), pltpu.VMEM((n, 1, 128), F32),
                pltpu.VMEM((ngx, ngy, 128), F32), pltpu.VMEM((16, nz), F32),
                pltpu.VMEM((nz, 128), jnp.bfloat16), pltpu.VMEM((128, nz), jnp.bfloat16),
                brick, brick,
                pltpu.SemaphoreType.DMA((8,)),
                pltpu.SemaphoreType.DMA((20,)), pltpu.SemaphoreType.DMA((20,)),
                pltpu.SemaphoreType.DMA((2,)), pltpu.SemaphoreType.DMA((2,)),
            ],
            compiler_params=pltpu.CompilerParams(
                collective_id=0, has_side_effects=True, vmem_limit_bytes=48 << 20
            ),
        )(perm, storage, source, weight, block_map, matrix)

    fine = P("gx", "gy", None)
    return jax.shard_map(
        shards,
        mesh=mesh,
        in_specs=(fine,) * 5 + (P(None, "gx", "gy", None),),
        out_specs=(fine, fine),
        check_vma=False,
    )
```

time: 707 us -> 41.3 us (0.06)
  blocking collectives: 447 us -> 0 us
  starting transfers between devices: 93.5 us -> 0 us
  waiting for transfers between devices: 60.5 us -> 0 us
  local copies, waits for them, and re-layouts: 44.4 us -> 7.21 us
  Pallas kernels: 0 us -> 33 us
  matrix products: 24.2 us -> 0 us
  other arithmetic: 15.8 us -> 0 us
  between operations: 15.7 us -> 0.65 us
    psum x11 -> x0, blocking collectives: 447 us -> none  [the longest x6 241 us: squares(): return lax.psum(values, ('gx', 'gy'))]
    ppermute x40 -> x0, starting transfers between devices: 93.5 us -> none  [the longest x20 67.7 us: padded_2(): before = lax.ppermute(last, axis, up)]
    ppermute x40 -> x0, waiting for transfers between devices: 60.5 us -> none  [the longest x20 53.3 us: padded_2(): after = lax.ppermute(initial, axis, down)]
    pallas_call x0 -> x1, Pallas kernels: none -> 33 us  [shards(): pl.pallas_call(functools.partial(kernel, ngx, ngy, block), out_shape=(sha...]
    dot_general x20 -> x0, matrix products: 24.2 us -> none  [the longest x10 18.2 us: accumulate(): jnp.dot(pair[0], indicator, precision=lax.Precision.HIGHEST)]
    dynamic_slice x20 -> x0, local copies, waits for them, and re-layouts: 20.2 us -> none  [block_sums(): lax.scan(accumulate, jnp.zeros((blocks,), jnp.float32), (slab_values, sla...]
    dynamic_update_slice x10 -> x0, local copies, waits for them, and re-layouts: 17.1 us -> none  [block_spread(): unused, spread = lax.scan(expand, jnp.int32(0), slab_maps)]
    reduce_sum x12 -> x0, other arithmetic: 8.16 us -> none  [the longest x6 4.39 us: conjugate(): step_size = norm_now / curve_sum(jnp.sum(direction * applied))]
  transfers between devices with their start and end apart: 40 -> 0, of which waited for: 19 -> 0; matrix products, arithmetic and copies ran while one was open for 1% -> 0% of each run, Pallas kernels for 0% -> 0%
where the time goes in v1:
time: 41.3 us; the launch traced here: 40.9 us
  Pallas kernels  33 us (80%)
  local copies, waits for them, and re-layouts  7.21 us (17%)
  between operations  0.65 us (2%)
    pallas_call x1, Pallas kernels, shards(): pl.pallas_call(functools.partial(kernel, ngx, ngy, block), out_shape=(sha...  33 us
    unnamed x14, local copies, waits for them, and re-layouts  7.21 us

profile of v1, /device:TPU:0, one launch (start us, length us, event | category | flops | bytes accessed | tf_op | source)
XLA Modules:
  0.0 40.9 jit_solution(7313888713576896964)
XLA Ops:
  0.6 0.0 copy-start
  0.6 1.0 %copy-done = f32[10,10,640]{2,1,0:T(8,128)S(1)} copy-done((f32[10,10,640]{2,1,0:T(8,128)S(1)}, f32[10,10,640]{2,1,0:T(8,128)}, u32[]{:S(2)}) %copy-start) | copy-done | bytes 256024
  1.6 0.0 copy-start.1
  1.6 1.0 %copy-done.1 = f32[10,10,640]{2,1,0:T(8,128)S(1)} copy-done((f32[10,10,640]{2,1,0:T(8,128)S(1)}, f32[10,10,640]{2,1,0:T(8,128)}, u32[]{:S(2)}) %copy-start.1) | copy-done | bytes 256024
  2.6 0.0 copy-start.2
  2.6 1.0 %copy-done.2 = f32[10,10,640]{2,1,0:T(8,128)S(1)} copy-done((f32[10,10,640]{2,1,0:T(8,128)S(1)}, f32[10,10,640]{2,1,0:T(8,128)}, u32[]{:S(2)}) %copy-start.2) | copy-done | bytes 256024
  3.6 0.0 copy-start.3
  3.6 1.0 %copy-done.3 = f32[10,10,640]{2,1,0:T(8,128)S(1)} copy-done((f32[10,10,640]{2,1,0:T(8,128)S(1)}, f32[10,10,640]{2,1,0:T(8,128)}, u32[]{:S(2)}) %copy-start.3) | copy-done | bytes 256024
  4.6 0.0 copy-start.4
  4.6 1.0 %copy-done.4 = s32[10,10,640]{2,1,0:T(8,128)S(1)} copy-done((s32[10,10,640]{2,1,0:T(8,128)S(1)}, s32[10,10,640]{2,1,0:T(8,128)}, u32[]{:S(2)}) %copy-start.4) | copy-done | bytes 256024
  5.6 0.0 copy-start.5
  5.6 0.7 %copy-done.5 = f32[27,1,1,64]{3,2,1,0:T(1,128)S(1)} copy-done((f32[27,1,1,64]{3,2,1,0:T(1,128)S(1)}, f32[27,1,1,64]{3,2,1,0:T(1,128)}, u32[]{:S(2)}) %copy-start.5) | copy-done | bytes 6936
  6.4 33.0 %shard_map.77 = (f32[10,10,640]{2,1,0:T(8,128)S(1)}, f32[10,10,640]{2,1,0:T(8,128)S(1)}) custom-call(f32[10,10,640]{2,1,0:T(8,128)S(1)} %copy-done, f32[10,10,640]{2,1,0:T(8,128)S(1)} %copy-done.1, f32[10,10,640]{2,1,0:T(8,128)S(1)} %copy-done.2, f32[10,10,640]{2,1,0:T(8,128)S(1)} %copy-done.3, s32[10,10,640]{2,1,0:T(8,128)S(1)} %copy-done.4, ...), custom_call_target="tpu_custom_call" | custom-call | tf_op jit(solution)/shard_map/pallas_call | solution.py:423
  39.4 0.8 %copy.10 = f32[10,10,640]{2,1,0:T(8,128)} copy(f32[10,10,640]{2,1,0:T(8,128)S(1)} %get-tuple-element.4) | data formatting | bytes 512000
  40.2 0.8 %copy.11 = f32[10,10,640]{2,1,0:T(8,128)} copy(f32[10,10,640]{2,1,0:T(8,128)S(1)} %get-tuple-element.5) | data formatting | bytes 512000
Async XLA Ops:
  0.6 1.0 %copy-start = (f32[10,10,640]{2,1,0:T(8,128)S(1)}, f32[10,10,640]{2,1,0:T(8,128)}, u32[]{:S(2)}) copy-start(f32[10,10,640]{2,1,0:T(8,128)} %perm_h.1) | copy-start | bytes 768004
  1.6 1.0 %copy-start.1 = (f32[10,10,640]{2,1,0:T(8,128)S(1)}, f32[10,10,640]{2,1,0:T(8,128)}, u32[]{:S(2)}) copy-start(f32[10,10,640]{2,1,0:T(8,128)} %storage_h.1) | copy-start | bytes 768004
  2.6 1.0 %copy-start.2 = (f32[10,10,640]{2,1,0:T(8,128)S(1)}, f32[10,10,640]{2,1,0:T(8,128)}, u32[]{:S(2)}) copy-start(f32[10,10,640]{2,1,0:T(8,128)} %source_h.1) | copy-start | bytes 768004
  3.6 1.0 %copy-start.3 = (f32[10,10,640]{2,1,0:T(8,128)S(1)}, f32[10,10,640]{2,1,0:T(8,128)}, u32[]{:S(2)}) copy-start(f32[10,10,640]{2,1,0:T(8,128)} %weight_h.1) | copy-start | bytes 768004
  4.6 1.0 %copy-start.4 = (s32[10,10,640]{2,1,0:T(8,128)S(1)}, s32[10,10,640]{2,1,0:T(8,128)}, u32[]{:S(2)}) copy-start(s32[10,10,640]{2,1,0:T(8,128)} %map_h.1) | copy-start | bytes 768004
  5.6 0.7 %copy-start.5 = (f32[27,1,1,64]{3,2,1,0:T(1,128)S(1)}, f32[27,1,1,64]{3,2,1,0:T(1,128)}, u32[]{:S(2)}) copy-start(f32[27,1,1,64]{3,2,1,0:T(1,128)} %matrix_h.1) | copy-start | bytes 20740

commit v2 on v1

--- a/solution.py
+++ b/solution.py
@@ -445,7 +445,7 @@
                 pltpu.SemaphoreType.DMA((2,)), pltpu.SemaphoreType.DMA((2,)),
             ],
             compiler_params=pltpu.CompilerParams(
-                collective_id=0, has_side_effects=True, vmem_limit_bytes=48 << 20
+                collective_id=0, has_side_effects=True, vmem_limit_bytes=63 << 20
             ),
         )(perm, storage, source, weight, block_map, matrix)
 

time: 41.3 us -> 35.7 us (0.86)
  local copies, waits for them, and re-layouts: 7.21 us -> 2.59 us
  Pallas kernels: 33 us -> 32.3 us
    unnamed x14 -> x4, local copies, waits for them, and re-layouts: 7.21 us -> 2.59 us
    pallas_call x1, Pallas kernels: 33 us -> 32.3 us  [shards(): pl.pallas_call(functools.partial(kernel, ngx, ngy, block), out_shape=(sha...]
where the time goes in v2:
time: 35.7 us; the launch traced here: 35.5 us
  Pallas kernels  32.3 us (90%)
  local copies, waits for them, and re-layouts  2.59 us (7%)
  between operations  0.65 us (2%)
    pallas_call x1, Pallas kernels, shards(): pl.pallas_call(functools.partial(kernel, ngx, ngy, block), out_shape=(sha...  32.3 us
    unnamed x4, local copies, waits for them, and re-layouts  2.59 us

profile of v2, /device:TPU:0, one launch (start us, length us, event | category | flops | bytes accessed | tf_op | source)
XLA Modules:
  0.0 35.5 jit_solution(3057548033151603673)
XLA Ops:
  0.6 32.3 %shard_map.77 = (f32[10,10,640]{2,1,0:T(8,128)}, f32[10,10,640]{2,1,0:T(8,128)}) custom-call(f32[10,10,640]{2,1,0:T(8,128)} %perm_h.1, f32[10,10,640]{2,1,0:T(8,128)} %storage_h.1, f32[10,10,640]{2,1,0:T(8,128)} %source_h.1, f32[10,10,640]{2,1,0:T(8,128)} %weight_h.1, s32[10,10,640]{2,1,0:T(8,128)} %map_h.1, f32[27,1,1,64]{3,2,1,0:T(1,128)} %matrix_h.1), custom_call_target="tpu_custom_call" | custom-call | tf_op jit(solution)/shard_map/pallas_call | solution.py:423
  32.9 0.0 copy-start
  33.0 1.8 %copy.10 = f32[10,10,640]{2,1,0:T(8,128)} copy(f32[10,10,640]{2,1,0:T(8,128)} %get-tuple-element.4) | data formatting | bytes 512000
  34.8 0.0 copy-done
  34.8 0.8 %copy.11 = f32[10,10,640]{2,1,0:T(8,128)} copy(f32[10,10,640]{2,1,0:T(8,128)S(1)} %copy-done) | data formatting | bytes 512000
Async XLA Ops:
  32.9 1.8 %copy-start = (f32[10,10,640]{2,1,0:T(8,128)S(1)}, f32[10,10,640]{2,1,0:T(8,128)}, u32[]{:S(2)}) copy-start(f32[10,10,640]{2,1,0:T(8,128)} %get-tuple-element.5) | copy-start | bytes 768004

commit v3 on v2

--- a/solution.py
+++ b/solution.py
@@ -53,15 +53,25 @@
     for load in loads:
         load.start()
 
-    def other(k):
-        t = lax.rem(me + k, n)
-        return (t // ngy, lax.rem(t, ngy))
+    def around(at, step, size):
+        moved_on = at + step
+        return jnp.where(moved_on >= size, moved_on - size, moved_on)
+
+    def for_others(act):
+        steps = [(a, b) for a in range(ngx) for b in range(ngy) if a or b]
+        if n <= 64:
+            steps.sort(key=lambda step: -min(step[1], ngy - step[1]))
+            for a, b in steps:
+                act((around(gx, a, ngx), around(gy, b, ngy)))
+        else:
+            @pl.loop(1, n)
+            def _(k):
+                t = lax.rem(me + k, n)
+                act((t // ngy, lax.rem(t, ngy)))
 
     barrier = pltpu.get_barrier_semaphore()
 
-    @pl.loop(1, n)
-    def _(k):
-        pl.semaphore_signal(barrier, inc=1, device_id=other(k), device_id_type=MESH)
+    for_others(lambda t: pl.semaphore_signal(barrier, inc=1, device_id=t, device_id_type=MESH))
 
     for d in range(2):
         @pl.when(jnp.logical_not(has[d]))
@@ -78,10 +88,13 @@
             for v in (v1, v2):
                 v[d * (cx + 1)] = jnp.zeros(v.shape[1:], F32)
 
-    zid = lax.broadcasted_iota(jnp.int32, (nz, 128), 0) // block
-    ind[...] = (zid == lax.broadcasted_iota(jnp.int32, (nz, 128), 1)).astype(F32).astype(jnp.bfloat16)
-    zidt = lax.broadcasted_iota(jnp.int32, (128, nz), 1) // block
-    indt[...] = (zidt == lax.broadcasted_iota(jnp.int32, (128, nz), 0)).astype(F32).astype(jnp.bfloat16)
+    def inside(shape, z_dim):
+        z = lax.broadcasted_iota(jnp.int32, shape, z_dim)
+        offset = z - block * lax.broadcasted_iota(jnp.int32, shape, 1 - z_dim)
+        return ((offset >= 0) & (offset < block)).astype(F32).astype(jnp.bfloat16)
+
+    ind[...] = inside((nz, 128), 0)
+    indt[...] = inside((128, nz), 1)
     pad_p[...] = jnp.ones(pad_p.shape, F32)
     tile[...] = jnp.zeros(tile.shape, F32)
     sx[...] = jnp.zeros(sx.shape, F32)
@@ -141,11 +154,11 @@
         tile[p : p + 1, 0:blocks] = matrix_v[p, 0]
         tile[p : p + 1, 64 : 64 + blocks] = matrix_v[p + 7, 0]
 
-    def matrix_copy(k):
+    def matrix_copy(target):
         return pltpu.make_async_remote_copy(
             src_ref=tile, dst_ref=gm.at[pl.ds(pl.multiple_of(me * 8, 8), 8)],
             send_sem=gsend_sem.at[0], recv_sem=grecv_sem.at[0],
-            device_id=other(k), device_id_type=MESH,
+            device_id=target, device_id_type=MESH,
         )
 
     loads[4].wait()
@@ -165,6 +178,12 @@
 
     for d in range(4):
         wait_halo(0, d, ry.at[0, d] if d < 2 else px.at[d - 2])
+
+    for d in range(2):
+        go(3, d, sy.at[3, d], ry.at[3, d ^ 1])
+        go(4, d, sym.at[d], rym.at[d ^ 1])
+        go(3, 2 + d, weight_h.at[(cx - 1) * d], wx.at[d ^ 1])
+        go(4, 2 + d, map_h.at[(cx - 1) * d], mx.at[d ^ 1])
 
     def to_rows(buffer, stage):
         @pl.loop(0, cx)
@@ -221,9 +240,7 @@
 
     field_halo(1, v1)
 
-    @pl.loop(1, n)
-    def _(k):
-        matrix_copy(k).start()
+    for_others(lambda t: matrix_copy(t).start())
 
     gm[pl.ds(pl.multiple_of(me * 8, 8), 8)] = tile[...]
 
@@ -240,22 +257,20 @@
 
     field_halo(2, v2)
 
-    for d in range(2):
-        go(3, d, sy.at[3, d], ry.at[3, d ^ 1])
-        go(4, d, sym.at[d], rym.at[d ^ 1])
-        go(3, 2 + d, weight_h.at[(cx - 1) * d], wx.at[d ^ 1])
-        go(4, 2 + d, map_h.at[(cx - 1) * d], mx.at[d ^ 1])
-
     field_wait(2, v2)
     to_rows(v2, 2)
 
-    zblock = lax.broadcasted_iota(jnp.int32, (cy, nz), 1) // block
+    zline = lax.broadcasted_iota(jnp.int32, (cy, nz), 1)
+
+    def is_here(cell_map):
+        return zline - block * cell_map < block
+
 
     def gather(x, carry):
         same, before = carry
         c, image = operate(v2, x)
         value = weight_v[x] * (source_v[x] - image)
-        here = map_v[x] == zblock
+        here = is_here(map_v[x])
         return same + jnp.where(here, value, 0.0), before + jnp.where(here, 0.0, value)
 
     zero = jnp.zeros((cy, nz), F32)
@@ -269,16 +284,14 @@
     mine = jnp.sum(sums, axis=0, keepdims=True)
     row[...] = mine
 
-    def row_copy(k):
+    def row_copy(target):
         return pltpu.make_async_remote_copy(
             src_ref=row, dst_ref=gr.at[me],
             send_sem=gsend_sem.at[1], recv_sem=grecv_sem.at[1],
-            device_id=other(k), device_id_type=MESH,
+            device_id=target, device_id_type=MESH,
         )
 
-    @pl.loop(1, n)
-    def _(k):
-        row_copy(k).start()
+    for_others(lambda t: row_copy(t).start())
 
     gr[me] = mine
 
@@ -287,7 +300,7 @@
         return pltpu.make_async_remote_copy(
             src_ref=part, dst_ref=part,
             send_sem=gsend_sem.at[which], recv_sem=grecv_sem.at[which],
-            device_id=other(1), device_id_type=MESH,
+            device_id=(around(gx, 1, ngx), gy), device_id_type=MESH,
         )
 
     all_of(gm, (n - 1) * 8, 0).wait_recv()
@@ -373,16 +386,16 @@
 
     for d in range(2):
         now, prior = by_block(1 + d)
-        ry[2, d] = ry[2, d] + ry[3, d] * jnp.where(rym[d] == zblock, now, prior)
+        ry[2, d] = ry[2, d] + ry[3, d] * jnp.where(is_here(rym[d]), now, prior)
         now, prior = by_block(3 + d)
         at = d * (cx + 1)
-        v1[at, 0:cy] = v2[at, 0:cy] + wx[d] * jnp.where(mx[d] == zblock, now, prior)
+        v1[at, 0:cy] = v2[at, 0:cy] + wx[d] * jnp.where(is_here(mx[d]), now, prior)
 
     now, prior = by_block(0)
 
     @pl.loop(0, cx)
     def _(x):
-        value = v2[x + 1, 0:cy] + weight_v[x] * jnp.where(map_v[x] == zblock, now, prior)
+        value = v2[x + 1, 0:cy] + weight_v[x] * jnp.where(is_here(map_v[x]), now, prior)
         pressure_v[x] = value
 
     out = pltpu.make_async_copy(pressure_v, pressure_h, local_sem.at[6])

time: 35.7 us -> 35.7 us (level)
  no operation moved by 1% of the time
where the time goes in v3:
time: 35.7 us; the launch traced here: 35.5 us
  Pallas kernels  32.3 us (90%)
  local copies, waits for them, and re-layouts  2.59 us (7%)
  between operations  0.65 us (2%)
    pallas_call x1, Pallas kernels, shards(): pl.pallas_call(functools.partial(kernel, ngx, ngy, block), out_shape=(sha...  32.3 us
    unnamed x4, local copies, waits for them, and re-layouts  2.59 us

profile of v3, /device:TPU:0, one launch (start us, length us, event | category | flops | bytes accessed | tf_op | source)
XLA Modules:
  0.0 35.5 jit_solution(17797768694052922301)
XLA Ops:
  0.6 32.3 %shard_map.77 = (f32[10,10,640]{2,1,0:T(8,128)}, f32[10,10,640]{2,1,0:T(8,128)}) custom-call(f32[10,10,640]{2,1,0:T(8,128)} %perm_h.1, f32[10,10,640]{2,1,0:T(8,128)} %storage_h.1, f32[10,10,640]{2,1,0:T(8,128)} %source_h.1, f32[10,10,640]{2,1,0:T(8,128)} %weight_h.1, s32[10,10,640]{2,1,0:T(8,128)} %map_h.1, f32[27,1,1,64]{3,2,1,0:T(1,128)} %matrix_h.1), custom_call_target="tpu_custom_call" | custom-call | tf_op jit(solution)/shard_map/pallas_call | solution.py:436
  32.9 0.0 copy-start
  32.9 1.8 %copy.10 = f32[10,10,640]{2,1,0:T(8,128)} copy(f32[10,10,640]{2,1,0:T(8,128)} %get-tuple-element.4) | data formatting | bytes 512000
  34.8 0.0 copy-done
  34.8 0.8 %copy.11 = f32[10,10,640]{2,1,0:T(8,128)} copy(f32[10,10,640]{2,1,0:T(8,128)S(1)} %copy-done) | data formatting | bytes 512000
Async XLA Ops:
  32.9 1.8 %copy-start = (f32[10,10,640]{2,1,0:T(8,128)S(1)}, f32[10,10,640]{2,1,0:T(8,128)}, u32[]{:S(2)}) copy-start(f32[10,10,640]{2,1,0:T(8,128)} %get-tuple-element.5) | copy-start | bytes 768004

commit v4 on v3

--- a/solution.py
+++ b/solution.py
@@ -35,11 +35,9 @@
     pressure_v, final_v,
     local_sem, send_sem, recv_sem, gsend_sem, grecv_sem,
 ):
-    n = ngx * ngy
     cx, cy, nz = perm_v.shape
     blocks = matrix_v.shape[-1]
     gx, gy = lax.axis_index("gx"), lax.axis_index("gy")
-    me = gx * ngy + gy
     has = (gy > 0, gy < ngy - 1, gx > 0, gx < ngx - 1)
     near = ((gx, gy - 1), (gx, gy + 1), (gx - 1, gy), (gx + 1, gy))
 
@@ -57,21 +55,13 @@
         moved_on = at + step
         return jnp.where(moved_on >= size, moved_on - size, moved_on)
 
-    def for_others(act):
-        steps = [(a, b) for a in range(ngx) for b in range(ngy) if a or b]
-        if n <= 64:
-            steps.sort(key=lambda step: -min(step[1], ngy - step[1]))
-            for a, b in steps:
-                act((around(gx, a, ngx), around(gy, b, ngy)))
-        else:
-            @pl.loop(1, n)
-            def _(k):
-                t = lax.rem(me + k, n)
-                act((t // ngy, lax.rem(t, ngy)))
+    along_x = [(around(gx, a, ngx), gy) for a in range(1, ngx)]
+    along_y = [(gx, around(gy, b, ngy)) for b in range(1, ngy)]
 
     barrier = pltpu.get_barrier_semaphore()
 
-    for_others(lambda t: pl.semaphore_signal(barrier, inc=1, device_id=t, device_id_type=MESH))
+    for t in along_x + along_y:
+        pl.semaphore_signal(barrier, inc=1, device_id=t, device_id_type=MESH)
 
     for d in range(2):
         @pl.when(jnp.logical_not(has[d]))
@@ -99,7 +89,7 @@
     tile[...] = jnp.zeros(tile.shape, F32)
     sx[...] = jnp.zeros(sx.shape, F32)
 
-    pl.semaphore_wait(barrier, n - 1)
+    pl.semaphore_wait(barrier, ngx + ngy - 2)
 
     def halo(stage, d, src, dst):
         return pltpu.make_async_remote_copy(
@@ -154,12 +144,26 @@
         tile[p : p + 1, 0:blocks] = matrix_v[p, 0]
         tile[p : p + 1, 64 : 64 + blocks] = matrix_v[p + 7, 0]
 
-    def matrix_copy(target):
+    def gather_copy(ref, which, target):
         return pltpu.make_async_remote_copy(
-            src_ref=tile, dst_ref=gm.at[pl.ds(pl.multiple_of(me * 8, 8), 8)],
-            send_sem=gsend_sem.at[0], recv_sem=grecv_sem.at[0],
+            src_ref=ref[0], dst_ref=ref[1],
+            send_sem=gsend_sem.at[which], recv_sem=grecv_sem.at[which],
             device_id=target, device_id_type=MESH,
         )
+
+    tile_rows = gm.at[pl.ds(pl.multiple_of((gy * ngx + gx) * 8, 8), 8)]
+    line_rows = gm.at[pl.ds(pl.multiple_of(gy * ngx * 8, 8), ngx * 8)]
+    matrix_x = ((tile, tile_rows), 0, gm.at[pl.ds(0, (ngx - 1) * 8)])
+    matrix_y = ((line_rows, line_rows), 1, gm.at[pl.ds(0, (ngy - 1) * ngx * 8)])
+    sums_x = ((row, gr.at[gy, gx]), 2, gr.at[0, pl.ds(0, ngx - 1)])
+    sums_y = ((gr.at[gy], gr.at[gy]), 3, gr.at[pl.ds(0, ngy - 1)])
+
+    def start_all(plan, targets):
+        for t in targets:
+            gather_copy(plan[0], plan[1], t).start()
+
+    def whole(plan):
+        return gather_copy((plan[2], plan[2]), plan[1], along_y[0])
 
     loads[4].wait()
     loads[5].wait()
@@ -240,9 +244,8 @@
 
     field_halo(1, v1)
 
-    for_others(lambda t: matrix_copy(t).start())
-
-    gm[pl.ds(pl.multiple_of(me * 8, 8), 8)] = tile[...]
+    start_all(matrix_x, along_x)
+    tile_rows[...] = tile[...]
 
     field_wait(1, v1)
     to_rows(v1, 1)
@@ -256,6 +259,9 @@
         sy[2, 1, pl.ds(x, 1)] = second[cy - 1 : cy]
 
     field_halo(2, v2)
+
+    whole(matrix_x).wait_recv()
+    start_all(matrix_y, along_y)
 
     field_wait(2, v2)
     to_rows(v2, 2)
@@ -284,30 +290,16 @@
     mine = jnp.sum(sums, axis=0, keepdims=True)
     row[...] = mine
 
-    def row_copy(target):
-        return pltpu.make_async_remote_copy(
-            src_ref=row, dst_ref=gr.at[me],
-            send_sem=gsend_sem.at[1], recv_sem=grecv_sem.at[1],
-            device_id=target, device_id_type=MESH,
-        )
-
-    for_others(lambda t: row_copy(t).start())
-
-    gr[me] = mine
-
-    def all_of(buffer, size, which):
-        part = buffer.at[pl.ds(0, size)]
-        return pltpu.make_async_remote_copy(
-            src_ref=part, dst_ref=part,
-            send_sem=gsend_sem.at[which], recv_sem=grecv_sem.at[which],
-            device_id=(around(gx, 1, ngx), gy), device_id_type=MESH,
-        )
-
-    all_of(gm, (n - 1) * 8, 0).wait_recv()
+    start_all(sums_x, along_x)
+    gr[gy, gx] = mine
+    whole(sums_x).wait_recv()
+    start_all(sums_y, along_y)
+
+    whole(matrix_y).wait_recv()
     lower = lax.broadcasted_iota(jnp.int32, (ngy, 128), 1) < 64
     for p in range(7):
         for g in range(ngx):
-            both = gm[pl.ds(g * ngy * 8 + p, ngy, stride=8), :]
+            both = gm[pl.ds(g * 8 + p, ngy, stride=ngx * 8), :]
             coef[p, g] = jnp.where(lower, both, 0.0)
             coef[p + 7, g] = jnp.where(lower, pltpu.roll(both, 64, 1), 0.0)
 
@@ -323,10 +315,10 @@
         for g in range(ngx):
             coef[26 - o, g] = moved(coef[o, (g - dx) % ngx], dy, dz)
 
-    all_of(gr, n - 1, 1).wait_recv()
+    whole(sums_y).wait_recv()
     for g in range(ngx):
         for h in range(ngy):
-            field[g, h : h + 1] = gr[g * ngy + h]
+            field[g, h : h + 1] = gr[h, g]
 
     def apply(u):
         result = [None] * ngx
@@ -416,8 +408,8 @@
 
     out2 = pltpu.make_async_copy(final_v, final_h, local_sem.at[7])
     out2.start()
-    all_of(gm, (n - 1) * 8, 0).wait_send()
-    all_of(gr, n - 1, 1).wait_send()
+    for plan in (matrix_x, matrix_y, sums_x, sums_y):
+        whole(plan).wait_send()
     out.wait()
     out2.wait()
 
@@ -449,13 +441,13 @@
                 face, face, pltpu.VMEM((2, cy, nz), jnp.int32),
                 pltpu.VMEM((8, 128), F32), pltpu.VMEM((n * 8, 128), F32),
                 pltpu.VMEM((27, ngx, ngy, 128), F32),
-                pltpu.VMEM((1, 128), F32), pltpu.VMEM((n, 1, 128), F32),
+                pltpu.VMEM((1, 128), F32), pltpu.VMEM((ngy, ngx, 1, 128), F32),
                 pltpu.VMEM((ngx, ngy, 128), F32), pltpu.VMEM((16, nz), F32),
                 pltpu.VMEM((nz, 128), jnp.bfloat16), pltpu.VMEM((128, nz), jnp.bfloat16),
                 brick, brick,
                 pltpu.SemaphoreType.DMA((8,)),
                 pltpu.SemaphoreType.DMA((20,)), pltpu.SemaphoreType.DMA((20,)),
-                pltpu.SemaphoreType.DMA((2,)), pltpu.SemaphoreType.DMA((2,)),
+                pltpu.SemaphoreType.DMA((4,)), pltpu.SemaphoreType.DMA((4,)),
             ],
             compiler_params=pltpu.CompilerParams(
                 collective_id=0, has_side_effects=True, vmem_limit_bytes=63 << 20

time: 35.7 us -> 35.3 us (0.989)
  Pallas kernels: 32.3 us -> 31.9 us
where the time goes in v4:
time: 35.3 us; the launch traced here: 35.2 us
  Pallas kernels  31.9 us (90%)
  local copies, waits for them, and re-layouts  2.59 us (7%)
  between operations  0.65 us (2%)
    pallas_call x1, Pallas kernels, shards(): pl.pallas_call(functools.partial(kernel, ngx, ngy, block), out_shape=(sha...  31.9 us
    unnamed x4, local copies, waits for them, and re-layouts  2.59 us

profile of v4, /device:TPU:0, one launch (start us, length us, event | category | flops | bytes accessed | tf_op | source)
XLA Modules:
  0.0 35.2 jit_solution(8156974555180195803)
XLA Ops:
  0.6 31.9 %shard_map.77 = (f32[10,10,640]{2,1,0:T(8,128)}, f32[10,10,640]{2,1,0:T(8,128)}) custom-call(f32[10,10,640]{2,1,0:T(8,128)} %perm_h.1, f32[10,10,640]{2,1,0:T(8,128)} %storage_h.1, f32[10,10,640]{2,1,0:T(8,128)} %source_h.1, f32[10,10,640]{2,1,0:T(8,128)} %weight_h.1, s32[10,10,640]{2,1,0:T(8,128)} %map_h.1, f32[27,1,1,64]{3,2,1,0:T(1,128)} %matrix_h.1), custom_call_target="tpu_custom_call" | custom-call | tf_op jit(solution)/shard_map/pallas_call | solution.py:428
  32.6 0.0 copy-start
  32.6 1.8 %copy.10 = f32[10,10,640]{2,1,0:T(8,128)} copy(f32[10,10,640]{2,1,0:T(8,128)} %get-tuple-element.4) | data formatting | bytes 512000
  34.4 0.0 copy-done
  34.4 0.8 %copy.11 = f32[10,10,640]{2,1,0:T(8,128)} copy(f32[10,10,640]{2,1,0:T(8,128)S(1)} %copy-done) | data formatting | bytes 512000
Async XLA Ops:
  32.6 1.8 %copy-start = (f32[10,10,640]{2,1,0:T(8,128)S(1)}, f32[10,10,640]{2,1,0:T(8,128)}, u32[]{:S(2)}) copy-start(f32[10,10,640]{2,1,0:T(8,128)} %get-tuple-element.5) | copy-start | bytes 768004

commit v5 on v4

--- a/solution.py
+++ b/solution.py
@@ -36,6 +36,7 @@
     local_sem, send_sem, recv_sem, gsend_sem, grecv_sem,
 ):
     cx, cy, nz = perm_v.shape
+    half = cx // 2
     blocks = matrix_v.shape[-1]
     gx, gy = lax.axis_index("gx"), lax.axis_index("gy")
     has = (gy > 0, gy < ngy - 1, gx > 0, gx < ngx - 1)
@@ -91,39 +92,42 @@
 
     pl.semaphore_wait(barrier, ngx + ngy - 2)
 
-    def halo(stage, d, src, dst):
+    def mark(stage, d, part):
+        return 20 + stage * 2 + d if part else stage * 4 + d
+
+    def halo(stage, d, src, dst, part=0):
         return pltpu.make_async_remote_copy(
             src_ref=src, dst_ref=dst,
-            send_sem=send_sem.at[stage * 4 + d],
-            recv_sem=recv_sem.at[stage * 4 + (d ^ 1)],
+            send_sem=send_sem.at[mark(stage, d, part)],
+            recv_sem=recv_sem.at[mark(stage, d ^ 1, part)],
             device_id=near[d], device_id_type=MESH,
         )
 
-    def send(stage, d, src, dst):
+    def send(stage, d, src, dst, part=0):
         @pl.when(has[d])
         def _():
-            halo(stage, d, src, dst).start()
-
-    def wait_sent(stage, d, src, dst):
+            halo(stage, d, src, dst, part).start()
+
+    def wait_sent(stage, d, src, dst, part=0):
         @pl.when(has[d])
         def _():
-            halo(stage, d, src, dst).wait_send()
-
-    def wait_halo(stage, d, dst):
+            halo(stage, d, src, dst, part).wait_send()
+
+    def wait_halo(stage, d, dst, part=0):
         @pl.when(has[d])
         def _():
             pltpu.make_async_remote_copy(
                 src_ref=dst, dst_ref=dst,
-                send_sem=send_sem.at[stage * 4 + d],
-                recv_sem=recv_sem.at[stage * 4 + d],
+                send_sem=send_sem.at[mark(stage, d, part)],
+                recv_sem=recv_sem.at[mark(stage, d, part)],
                 device_id=near[d], device_id_type=MESH,
             ).wait_recv()
 
     sent = []
 
-    def go(stage, d, src, dst):
-        send(stage, d, src, dst)
-        sent.append((stage, d, src, dst))
+    def go(stage, d, src, dst, part=0):
+        send(stage, d, src, dst, part)
+        sent.append((stage, d, src, dst, part))
 
     for d in range(2):
         go(0, 2 + d, perm_h.at[(cx - 1) * d], px.at[d ^ 1])
@@ -133,8 +137,8 @@
     def _(x):
         p = perm_v[x]
         pad_p[x + 1, 0:cy] = p
-        sy[0, 0, pl.ds(x, 1)] = p[0:1]
-        sy[0, 1, pl.ds(x, 1)] = p[cy - 1 : cy]
+        sy[0, 0, x // half, pl.ds(x % half, 1)] = p[0:1]
+        sy[0, 1, x // half, pl.ds(x % half, 1)] = p[cy - 1 : cy]
 
     for d in range(2):
         go(0, d, sy.at[0, d], ry.at[0, d ^ 1])
@@ -171,11 +175,11 @@
     @pl.loop(0, cx)
     def _(x):
         w = weight_v[x]
-        sy[3, 0, pl.ds(x, 1)] = w[0:1]
-        sy[3, 1, pl.ds(x, 1)] = w[cy - 1 : cy]
+        sy[3, 0, x // half, pl.ds(x % half, 1)] = w[0:1]
+        sy[3, 1, x // half, pl.ds(x % half, 1)] = w[cy - 1 : cy]
         m = map_v[x]
-        sym[0, pl.ds(x, 1)] = m[0:1]
-        sym[1, pl.ds(x, 1)] = m[cy - 1 : cy]
+        sym[0, x // half, pl.ds(x % half, 1)] = m[0:1]
+        sym[1, x // half, pl.ds(x % half, 1)] = m[cy - 1 : cy]
 
     loads[2].wait()
     loads[3].wait()
@@ -189,11 +193,12 @@
         go(3, 2 + d, weight_h.at[(cx - 1) * d], wx.at[d ^ 1])
         go(4, 2 + d, map_h.at[(cx - 1) * d], mx.at[d ^ 1])
 
-    def to_rows(buffer, stage):
-        @pl.loop(0, cx)
-        def _(x):
-            buffer[x + 1, 15:16] = ry[stage, 0, pl.ds(x, 1)]
-            buffer[x + 1, cy : cy + 1] = ry[stage, 1, pl.ds(x, 1)]
+    def to_rows(buffer, stage, parts=(0, 1)):
+        for h in parts:
+            for i in range(half):
+                x = h * half + i + 1
+                buffer[x, 15:16] = ry[stage, 0, h, i : i + 1]
+                buffer[x, cy : cy + 1] = ry[stage, 1, h, i : i + 1]
 
     pad_p[0, 0:cy] = px[0]
     pad_p[cx + 1, 0:cy] = px[1]
@@ -202,8 +207,7 @@
     tx[0] = harmonic(pad_p[0], pad_p[1])
     lane = lax.broadcasted_iota(jnp.int32, (16, nz), 1)
 
-    @pl.loop(0, cx)
-    def _(x):
+    def faces(x, i, h):
         p = pad_p[x + 1]
         up = harmonic(p, pad_p[x + 2])
         tx[x + 1] = up
@@ -221,19 +225,28 @@
         inv[x] = inverse
         first = OMEGA * source_v[x] * inverse
         v1[x + 1, 0:cy] = first
-        sy[1, 0, pl.ds(x, 1)] = first[0:1]
-        sy[1, 1, pl.ds(x, 1)] = first[cy - 1 : cy]
-
-    def field_halo(stage, v):
+        sy[1, 0, h, pl.ds(i, 1)] = first[0:1]
+        sy[1, 1, h, pl.ds(i, 1)] = first[cy - 1 : cy]
+
+    def halves(act, stage, v, before=None):
+        for h in range(2):
+            if before is not None:
+                before(h)
+
+            @pl.loop(0, half)
+            def _(i):
+                act(h * half + i, i, h)
+
+            for d in range(2):
+                go(stage, d, sy.at[stage, d, h], ry.at[stage, d ^ 1, h], h)
+            sx[stage - 1, h, 0:cy] = v[1 + (cx - 1) * h, 0:cy]
+            go(stage, 2 + h, sx.at[stage - 1, h], v.at[(cx + 1) * (1 - h)])
+
+    def field_wait(stage, v, h):
         for d in range(2):
-            go(stage, d, sy.at[stage, d], ry.at[stage, d ^ 1])
-        for d in range(2):
-            sx[stage - 1, d, 0:cy] = v[1 + (cx - 1) * d, 0:cy]
-            go(stage, 2 + d, sx.at[stage - 1, d], v.at[(cx + 1) * (1 - d)])
-
-    def field_wait(stage, v):
-        for d in range(4):
-            wait_halo(stage, d, ry.at[stage, d] if d < 2 else v.at[(cx + 1) * (d - 2)])
+            wait_halo(stage, d, ry.at[stage, d, h], h)
+        wait_halo(stage, 2 + h, v.at[(cx + 1) * h])
+        to_rows(v, stage, (h,))
 
     def operate(v, x):
         c = v[x + 1]
@@ -242,29 +255,22 @@
         total += tzp[x] * pltpu.roll(c, nz - 1, 1)[0:cy] + tzm[x] * pltpu.roll(c, 1, 1)[0:cy]
         return c[0:cy], diag[x] * c[0:cy] - total
 
-    field_halo(1, v1)
+    halves(faces, 1, v1)
 
     start_all(matrix_x, along_x)
     tile_rows[...] = tile[...]
 
-    field_wait(1, v1)
-    to_rows(v1, 1)
-
-    @pl.loop(0, cx)
-    def _(x):
+    def smooth(x, i, h):
         c, image = operate(v1, x)
         second = c + OMEGA * (source_v[x] - image) * inv[x]
         v2[x + 1, 0:cy] = second
-        sy[2, 0, pl.ds(x, 1)] = second[0:1]
-        sy[2, 1, pl.ds(x, 1)] = second[cy - 1 : cy]
-
-    field_halo(2, v2)
+        sy[2, 0, h, pl.ds(i, 1)] = second[0:1]
+        sy[2, 1, h, pl.ds(i, 1)] = second[cy - 1 : cy]
+
+    halves(smooth, 2, v2, lambda h: field_wait(1, v1, h))
 
     whole(matrix_x).wait_recv()
     start_all(matrix_y, along_y)
-
-    field_wait(2, v2)
-    to_rows(v2, 2)
 
     zline = lax.broadcasted_iota(jnp.int32, (cy, nz), 1)
 
@@ -280,7 +286,10 @@
         return same + jnp.where(here, value, 0.0), before + jnp.where(here, 0.0, value)
 
     zero = jnp.zeros((cy, nz), F32)
-    same, before = lax.fori_loop(0, cx, gather, (zero, zero))
+    field_wait(2, v2, 0)
+    carry = lax.fori_loop(0, half, gather, (zero, zero))
+    field_wait(2, v2, 1)
+    same, before = lax.fori_loop(half, cx, gather, carry)
     same = jnp.broadcast_to(jnp.sum(same, axis=0, keepdims=True), (16, nz))
     before = jnp.broadcast_to(jnp.sum(before, axis=0, keepdims=True), (16, nz))
     high, middle, low = pieces(same + pltpu.roll(before, nz - 1, 1))
@@ -378,7 +387,9 @@
 
     for d in range(2):
         now, prior = by_block(1 + d)
-        ry[2, d] = ry[2, d] + ry[3, d] * jnp.where(is_here(rym[d]), now, prior)
+        for h in range(2):
+            choice = jnp.where(zline[0:half] - block * rym[d, h] < block, now[0:half], prior[0:half])
+            ry[2, d, h] = ry[2, d, h] + ry[3, d, h] * choice
         now, prior = by_block(3 + d)
         at = d * (cx + 1)
         v1[at, 0:cy] = v2[at, 0:cy] + wx[d] * jnp.where(is_here(mx[d]), now, prior)
@@ -435,9 +446,9 @@
                 pltpu.VMEM(matrix.shape, F32),
                 padded, padded, padded, pltpu.VMEM((cx + 1, 16, nz), F32),
                 brick, brick, brick, brick, brick, brick,
-                pltpu.VMEM((4, 2, cx, nz), F32), pltpu.VMEM((4, 2, cx, nz), F32),
+                pltpu.VMEM((4, 2, 2, cx // 2, nz), F32), pltpu.VMEM((4, 2, 2, cx // 2, nz), F32),
                 pltpu.VMEM((2, 2, 16, nz), F32),
-                pltpu.VMEM((2, cx, nz), jnp.int32), pltpu.VMEM((2, cx, nz), jnp.int32),
+                pltpu.VMEM((2, 2, cx // 2, nz), jnp.int32), pltpu.VMEM((2, 2, cx // 2, nz), jnp.int32),
                 face, face, pltpu.VMEM((2, cy, nz), jnp.int32),
                 pltpu.VMEM((8, 128), F32), pltpu.VMEM((n * 8, 128), F32),
                 pltpu.VMEM((27, ngx, ngy, 128), F32),
@@ -446,7 +457,7 @@
                 pltpu.VMEM((nz, 128), jnp.bfloat16), pltpu.VMEM((128, nz), jnp.bfloat16),
                 brick, brick,
                 pltpu.SemaphoreType.DMA((8,)),
-                pltpu.SemaphoreType.DMA((20,)), pltpu.SemaphoreType.DMA((20,)),
+                pltpu.SemaphoreType.DMA((30,)), pltpu.SemaphoreType.DMA((30,)),
                 pltpu.SemaphoreType.DMA((4,)), pltpu.SemaphoreType.DMA((4,)),
             ],
             compiler_params=pltpu.CompilerParams(

time: 35.3 us -> 34.7 us (0.983)
  Pallas kernels: 31.9 us -> 31.3 us
    pallas_call x1, Pallas kernels: 31.9 us -> 31.3 us  [shards(): pl.pallas_call(functools.partial(kernel, ngx, ngy, block), out_shape=(sha...]
where the time goes in v5:
time: 34.7 us; the launch traced here: 34.6 us
  Pallas kernels  31.3 us (90%)
  local copies, waits for them, and re-layouts  2.59 us (7%)
  between operations  0.65 us (2%)
    pallas_call x1, Pallas kernels, shards(): pl.pallas_call(functools.partial(kernel, ngx, ngy, block), out_shape=(sha...  31.3 us
    unnamed x4, local copies, waits for them, and re-layouts  2.59 us

profile of v5, /device:TPU:0, one launch (start us, length us, event | category | flops | bytes accessed | tf_op | source)
XLA Modules:
  0.0 34.6 jit_solution(13384686627513414783)
XLA Ops:
  0.6 31.3 %shard_map.77 = (f32[10,10,640]{2,1,0:T(8,128)}, f32[10,10,640]{2,1,0:T(8,128)}) custom-call(f32[10,10,640]{2,1,0:T(8,128)} %perm_h.1, f32[10,10,640]{2,1,0:T(8,128)} %storage_h.1, f32[10,10,640]{2,1,0:T(8,128)} %source_h.1, f32[10,10,640]{2,1,0:T(8,128)} %weight_h.1, s32[10,10,640]{2,1,0:T(8,128)} %map_h.1, f32[27,1,1,64]{3,2,1,0:T(1,128)} %matrix_h.1), custom_call_target="tpu_custom_call" | custom-call | tf_op jit(solution)/shard_map/pallas_call | solution.py:439
  32.0 0.0 copy-start
  32.0 1.8 %copy.10 = f32[10,10,640]{2,1,0:T(8,128)} copy(f32[10,10,640]{2,1,0:T(8,128)} %get-tuple-element.4) | data formatting | bytes 512000
  33.8 0.0 copy-done
  33.8 0.8 %copy.11 = f32[10,10,640]{2,1,0:T(8,128)} copy(f32[10,10,640]{2,1,0:T(8,128)S(1)} %copy-done) | data formatting | bytes 512000
Async XLA Ops:
  32.0 1.8 %copy-start = (f32[10,10,640]{2,1,0:T(8,128)S(1)}, f32[10,10,640]{2,1,0:T(8,128)}, u32[]{:S(2)}) copy-start(f32[10,10,640]{2,1,0:T(8,128)} %get-tuple-element.5) | copy-start | bytes 768004
